TPU v7x, 32 devices: a whole 2x2x4 slice. The times are simulated.
32 devices in a mesh: col: 8 (over z, y), row: 4 (over x, core).
Axes of the slice: x: 2, y: 2, z: 4, core: 2. Of those that a mesh axis runs over, the one named last changes fastest.
Arguments:
- pivot_block: bfloat16 [512, 512], P(None, 'row'), may hold values from -0.5 to 5.5, as said below
- panel: bfloat16 [4, 256, 512], P('row', 'col'), may hold values from -1.1953125 to 1.1953125
- lead: int32 [4, 2], P('row'), may hold values from 0 to 3
- trailing: bfloat16 [1024, 1024], P('row', 'col'), may hold values from -1.796875 to 1.796875
Outputs:
- pivot_factor: float32 [512, 512], P(None, 'row')
- panel_factor: bfloat16 [4, 256, 512], P('row', 'col')
- schur: bfloat16 [1024, 1024], P('row', 'col')
Inputs may be any that keep to these rules, and one draw needn't show every extreme that they name: `pivot_block`: symmetric positive definite.
All inputs are finite; a program needn't handle non-finite values.
Results may differ from a plain program's by a relative error of at most 0.0042.
Values may be sent and summed in bfloat16 or wider, within the bound.
No kernel may reach another device: no remote copies, remote signals or barrier semaphores. Data moves between devices by JAX's collectives and lax.ppermute only.
A program may use at most 64 MiB of HBM per device.

v0:
```python
import functools

import jax
import jax.numpy as jnp
from jax import lax
from jax.experimental import pallas as pl
from jax.experimental.pallas import tpu as pltpu
from jax.sharding import PartitionSpec as P

BLOCK = 128
STRIP = 32
GROUP = 8
LANES = 128


def split(value):
    high = value.astype(jnp.bfloat16)
    low = (value - high.astype(jnp.float32)).astype(jnp.bfloat16)
    return high, low


def row_of(value, row):
    return jnp.broadcast_to(value[row : row + 1, :], (GROUP, LANES))


def reciprocal(value):
    guess = pl.reciprocal(value, approx=True)
    return guess, 2.0 - value * guess


def eliminate_strip(strip, first):
    groups = STRIP // GROUP
    sublane = lax.broadcasted_iota(jnp.int32, (GROUP, LANES), 0)
    lane = lax.broadcasted_iota(jnp.int32, (GROUP, LANES), 1)
    zero = jnp.zeros((GROUP, LANES), jnp.float32)
    diag = [strip[g * GROUP : (g + 1) * GROUP, :] for g in range(groups)]
    column = [
        [
            jnp.broadcast_to(diag[g][:, first + j : first + j + 1], (GROUP, LANES)) if g >= j // GROUP else None
            for g in range(groups)
        ]
        for j in range(STRIP)
    ]
    inside = (lane >= first) & (lane < first + STRIP)
    block = [jnp.where(inside, jnp.where(lane - first == sublane + g * GROUP, 1.0, 0.0), diag[g]) for g in range(groups)]
    lower = [zero] * groups
    for k in range(0, STRIP, 2):
        home, sub = k // GROUP, k % GROUP
        u, v = column[k], column[k + 1]
        a = row_of(u[home], sub)
        b = row_of(u[home], sub + 1)
        c = row_of(v[home], sub + 1)
        det = a * c - b * b
        guess, correction = reciprocal(det)
        n1 = [None if g < home else c * u[g] - b * v[g] for g in range(groups)]
        n2 = [None if g < home else a * v[g] - b * u[g] for g in range(groups)]
        w1 = [None if g < home else (n1[g] * guess) * correction for g in range(groups)]
        w2 = [None if g < home else (n2[g] * guess) * correction for g in range(groups)]
        for j in range(k + 2, STRIP):
            at, row = j // GROUP, j % GROUP
            uj, vj = row_of(u[at], row), row_of(v[at], row)
            for g in range(at, groups):
                if j < k + 4:
                    step = ((n1[g] * uj + n2[g] * vj) * guess) * correction
                else:
                    step = w1[g] * uj + w2[g] * vj
                column[j][g] = column[j][g] - step
        root_a = lax.rsqrt(a)
        root_d = lax.rsqrt(a * det)
        for g in range(home, groups):
            lower[g] = jnp.where(lane == first + k, u[g] * root_a, lower[g])
            lower[g] = jnp.where(lane == first + k + 1, n2[g] * root_d, lower[g])
        below = sublane > sub + 1
        w1[home] = jnp.where(below, w1[home], 0.0)
        w2[home] = jnp.where(below, w2[home], 0.0)
        t0, t1 = row_of(block[home], sub), row_of(block[home], sub + 1)
        for g in range(home, groups):
            block[g] = block[g] - (w1[g] * t0 + w2[g] * t1)
        block[home] = jnp.where(sublane == sub, t0 * root_a, block[home])
        block[home] = jnp.where(sublane == sub + 1, (a * t1 - b * t0) * root_d, block[home])
    for g in range(groups):
        keep = (lane <= first + sublane + g * GROUP) & inside
        lower[g] = jnp.where(keep, lower[g], 0.0)
    return jnp.concatenate(block, axis=0), jnp.concatenate(lower, axis=0)


def matmul(left, right):
    return jnp.dot(left, right, preferred_element_type=jnp.float32)


def stacked(value):
    high, low = split(value)
    return jnp.concatenate([high, high, low, jnp.zeros_like(high)], axis=0)


def factor_kernel(axis, *refs):
    count = lax.axis_size(axis)
    parts, (own_ref, high_ref, low_ref, work, lower) = refs[:count], refs[count:]
    me = lax.axis_index(axis)
    lane = lax.broadcasted_iota(jnp.int32, (LANES, LANES), 1)
    row = lax.broadcasted_iota(jnp.int32, (LANES, LANES), 0)
    beyond = lane // STRIP > row // STRIP
    for shift, part in enumerate(parts):
        work[lax.rem(me + shift, count), : count * LANES, :] = part[...].astype(jnp.float32)

    def rows_at(block):
        return pl.ds(pl.multiple_of(block * LANES, LANES), LANES)

    def update(target, left, rights, places, on):
        high, low = split(jnp.where(on, left.T, 0.0))
        both = jnp.concatenate([high, low], axis=1)
        for d, (place, (right_high, right_low)) in enumerate(zip(places, rights)):
            product = matmul(both, jnp.concatenate([right_high, right_high], axis=0)) + matmul(high, right_low)
            old = work[place, rows_at(target), :]
            if d == 0:
                old = jnp.where(on, 0.0, old)
            work[place, rows_at(target), :] = old - product

    def block_step(q, carry):
        places = [lax.rem(q + d, count) for d in range(count)]
        rows = [work[place, rows_at(q), :] for place in places]

        before = jnp.maximum(q - 1, 0)
        old_places = [lax.rem(before + d, count) for d in range(count)]
        rights = [work[place, rows_at(before), :] for place in old_places]
        rights[0] = jnp.where(beyond, 0.0, rights[0])
        rights = [split(right) for right in rights]
        for target in (q + 1, q + 2):
            update(target, work[target, rows_at(before), :], rights, old_places, q > 0)

        done = [[] for _ in places]
        for first in range(0, LANES, STRIP):
            last = first + STRIP
            solved, diagonal = eliminate_strip(rows[0][:STRIP], first)
            lower[q, first:last, :] = diagonal
            in_strip = (lane[:STRIP] >= first) & (lane[:STRIP] < last)
            high, low = split(jnp.where(in_strip, solved, 0.0))
            high, low = high.astype(jnp.float32), low.astype(jnp.float32)
            inverse = high if first == 0 else pltpu.roll(high, LANES - first, 1)
            inverse += pltpu.roll(low, (LANES + STRIP - first) % LANES, 1) if first != STRIP else low
            inverse += pltpu.roll(high, (LANES + 2 * STRIP - first) % LANES, 1) if first != 2 * STRIP else high
            inverse = inverse.astype(jnp.bfloat16)
            strips = [solved] + [matmul(inverse, stacked(part[:STRIP])) for part in rows[1:]]
            for part, strip in zip(done, strips):
                part.append(strip)
            if last == LANES:
                break
            high, low = split(solved)
            wide = jnp.concatenate([high, low, high, jnp.zeros_like(high)], axis=0).astype(jnp.float32)
            left = wide.T[last:, :].astype(jnp.bfloat16)
            under = [part[STRIP:] for part in rows]
            inside = (lane[last:] >= first) & (lane[last:] < last)
            under[0] = jnp.where(inside, 0.0, under[0])
            rows = [part - matmul(left, stacked(strip)) for part, strip in zip(under, strips)]

        done = [jnp.concatenate(part, axis=0) for part in done]
        for place, part in zip(places, done):
            work[place, rows_at(q), :] = part
        rights = [split(part) for part in [jnp.where(beyond, 0.0, done[0])] + done[1:]]
        update(q + 1, done[1], rights, places, True)
        return carry

    lax.fori_loop(0, count, block_step, 0)

    for i in range(count):
        block = work[i, rows_at(me), :]
        upper = jnp.where((i > me) | ((i == me) & beyond), block, 0.0)
        own_ref[i * LANES : (i + 1) * LANES, :] = upper.T + jnp.where(i == me, lower[i], 0.0)
        for c in range(count):
            block = work[c, i * LANES : (i + 1) * LANES, :]
            if c > i:
                block = jnp.zeros_like(block)
            elif c == i:
                block = jnp.where(lane <= row, block, 0.0)
            high, low = split(block)
            high_ref[i * LANES : (i + 1) * LANES, c * LANES : (c + 1) * LANES] = high
            low_ref[i * LANES : (i + 1) * LANES, c * LANES : (c + 1) * LANES] = low


def solve_kernel(row_axis, col_axis, order, group_count, *refs):
    high_ref, low_ref = refs[:2]
    inputs = refs[2 : 3 + group_count]
    trailing_ref, own_ref, schur_ref, group, side = refs[3 + group_count :]
    size = high_ref.shape[0]
    half = size // 2
    share = own_ref.shape[1]
    count = side.shape[0] // share
    my_row, my_col = lax.axis_index(row_axis), lax.axis_index(col_axis)
    for i, ref in enumerate(inputs[:-1]):
        if order is None:
            group[...] = ref[...]
        else:
            for p in range(count):
                at = jnp.bitwise_xor(my_col, i * count + p) * share
                group[pl.ds(pl.multiple_of(at, share), share), :] = ref[p * share : (p + 1) * share, :]
    for p in range(count):
        place = jnp.bitwise_xor(my_row, p) if order else lax.rem(my_row + count - p, count)
        side[pl.ds(pl.multiple_of(place * share, share), share), :] = inputs[-1][p * share : (p + 1) * share, :]
    contract = (((1,), (1,)), ((), ()))

    def product(left, right):
        return lax.dot_general(left, right, contract, preferred_element_type=jnp.float32)

    def solve(rows):
        first = product(rows[:, :half], high_ref[:half, :half]) + product(rows[:, :half], low_ref[:half, :half])
        second = product(rows, high_ref[half:, :]) + product(rows, low_ref[half:, :])
        return jnp.concatenate([first, second], axis=1).astype(jnp.bfloat16)

    side[...] = solve(side[...])
    rows = group.shape[0]
    chunk = min(rows, 256)

    def step(i, carry):
        here = pl.ds(pl.multiple_of(i * chunk, chunk), chunk)
        solved = solve(group[here, :])
        group[here, :] = solved
        update = product(solved, side[...])
        schur_ref[here, :] = (trailing_ref[here, :].astype(jnp.float32) - update).astype(jnp.bfloat16)
        return carry

    if rows == chunk:
        step(0, 0)
    else:
        lax.fori_loop(0, rows // chunk, step, 0)
    own_ref[0] = group[pl.ds(pl.multiple_of(my_col * share, share), share), :]


def body(pivot_block, panel, lead, trailing):
    pivot_size, local_width = pivot_block.shape
    rows, cols = lax.axis_size("row"), lax.axis_size("col")
    share = panel.shape[1]
    col_index = lax.axis_index("col")
    vmem = pl.BlockSpec(memory_space=pltpu.VMEM)

    pivots = [pivot_block] + [
        lax.ppermute(pivot_block, "row", [((d + s) % rows, d) for d in range(rows)]) for s in range(1, rows)
    ]

    def live(shards, rows_of):
        block = jnp.concatenate([(shard * share + jnp.arange(share)) // BLOCK for shard in shards])
        matches = block[:, None] == jnp.arange(lead.shape[1])[None, :]
        row_lead = jnp.sum(jnp.where(matches, lead, 0), axis=1)
        keep = (jnp.arange(pivot_size) // BLOCK)[None, :] >= row_lead[:, None]
        return jnp.where(keep, rows_of, jnp.zeros_like(rows_of))

    ratio = cols // rows
    paired = cols == 2 * rows and rows & (rows - 1) == 0

    def to_side(array, shift):
        pairs = []
        for r in range(rows):
            for c in range(cols):
                to_row, to_col = (c % rows + shift) % rows, r * ratio + c // rows
                pairs.append((c * rows + r, to_col * rows + to_row))
        return lax.ppermute(array, ("col", "row"), pairs)

    if paired:
        quad = [panel[0]] + [lax.ppermute(panel[0], "col", [(d ^ p, d) for d in range(cols)]) for p in range(1, rows)]
        quad = live([col_index ^ p for p in range(rows)], jnp.concatenate(quad, axis=0))
        group = [quad, lax.ppermute(quad, "col", [(d ^ rows, d) for d in range(cols)])]
        side = to_side(quad, 0)
    else:
        masked = live([col_index], panel[0])
        group = [lax.all_gather(masked, "col", axis=0, tiled=True)]
        side = jnp.concatenate([to_side(masked, s) for s in range(rows)], axis=0)

    own, high, low = pl.pallas_call(
        functools.partial(factor_kernel, "row"),
        out_shape=(
            jax.ShapeDtypeStruct((pivot_size, local_width), jnp.float32),
            jax.ShapeDtypeStruct((pivot_size, pivot_size), jnp.bfloat16),
            jax.ShapeDtypeStruct((pivot_size, pivot_size), jnp.bfloat16),
        ),
        in_specs=[vmem] * rows,
        out_specs=(vmem,) * 3,
        scratch_shapes=[
            pltpu.VMEM((rows + 2, pivot_size + 2 * LANES, LANES), jnp.float32),
            pltpu.VMEM((rows, LANES, LANES), jnp.float32),
        ],
        compiler_params=pltpu.CompilerParams(vmem_limit_bytes=32 * 1024 * 1024),
        cost_estimate=pl.CostEstimate(flops=10**9, bytes_accessed=2 * 10**6, transcendentals=10**5),
        name="factor",
    )(*pivots)

    group_rows = share * cols
    panel_factor, schur = pl.pallas_call(
        functools.partial(solve_kernel, "row", "col", True if paired else None, len(group)),
        out_shape=(
            jax.ShapeDtypeStruct(panel.shape, jnp.bfloat16),
            jax.ShapeDtypeStruct(trailing.shape, jnp.bfloat16),
        ),
        in_specs=[vmem] * (4 + len(group)),
        out_specs=(vmem,) * 2,
        scratch_shapes=[
            pltpu.VMEM((group_rows, pivot_size), jnp.bfloat16),
            pltpu.VMEM((share * rows, pivot_size), jnp.bfloat16),
        ],
        compiler_params=pltpu.CompilerParams(vmem_limit_bytes=48 * 1024 * 1024),
        cost_estimate=pl.CostEstimate(flops=4 * 10**8, bytes_accessed=2 * 10**6, transcendentals=0),
        name="solve",
    )(high, low, *group, side, trailing)
    return (own, panel_factor, schur)


def solution(mesh):
    return jax.shard_map(
        body,
        mesh=mesh,
        in_specs=(P(None, "row"), P("row", "col", None), P("row", None), P("row", "col")),
        out_specs=(P(None, "row"), P("row", "col", None), P("row", "col")),
        check_vma=False,
    )
```

profile of v0, /device:TPU:1, one launch (start us, length us, event | category | flops | bytes accessed | tf_op | source)
XLA Modules:
  0.0 35.8 jit_solution(13166415466971091182)
XLA Ops:
  0.6 0.0 copy-start.2
  0.6 0.1 collective-permute-start
  0.7 2.7 %collective-permute-start.1 = (bf16[512,128]{1,0:T(8,128)(2,1)}, bf16[512,128]{1,0:T(8,128)(2,1)S(1)}, u32[]{:S(2)}, u32[]{:S(2)}) collective-permute-start(bf16[512,128]{1,0:T(8,128)(2,1)} %refs_0_.1), channel_id=1, source_target_pairs={{2,0},{3,1},{0,2},{1,3},{6,4},{7,5},{4,6},{5,7},{10,8},{11,9},{8,1... | collective-permute-start | bytes 393224 | tf_op jit(solution)/shard_map/ppermute | solution.py:236
  3.4 2.3 %collective-permute-start.5 = (bf16[32,512]{1,0:T(8,128)(2,1)}, bf16[32,512]{1,0:T(8,128)(2,1)S(1)}, u32[]{:S(2)}, u32[]{:S(2)}) collective-permute-start(bf16[32,512]{1,0:T(8,128)(2,1)} %bitcast.2), channel_id=1, source_target_pairs={{12,0},{8,4},{4,8},{0,12},{28,16},{24,20},{20,24},{16,28},{13,1},{... | collective-permute-start | bytes 98312 | tf_op jit(solution)/shard_map/ppermute | solution.py:258
  5.7 0.2 collective-permute-start.4
  5.8 0.2 collective-permute-start.3
  6.1 0.1 pad_add_fusion
  6.2 0.7 %copy-done.3 = s32[1,2]{1,0:T(1,128)S(1)} copy-done((s32[1,2]{1,0:T(1,128)S(1)}, s32[1,2]{1,0:T(1,128)}, u32[]{:S(2)}) %copy-start.3) | copy-done | bytes 32
  6.8 0.1 fusion.3
  6.9 0.4 %collective-permute-done.5 = bf16[32,512]{1,0:T(8,128)(2,1)S(1)} collective-permute-done((bf16[32,512]{1,0:T(8,128)(2,1)}, bf16[32,512]{1,0:T(8,128)(2,1)S(1)}, u32[]{:S(2)}, u32[]{:S(2)}) %collective-permute-start.5) | collective-permute-done | bytes 32800 | tf_op jit(solution)/shard_map/ppermute | solution.py:258
  7.3 2.6 %collective-permute-start.2 = (bf16[512,128]{1,0:T(8,128)(2,1)}, bf16[512,128]{1,0:T(8,128)(2,1)S(1)}, u32[]{:S(2)}, u32[]{:S(2)}) collective-permute-start(bf16[512,128]{1,0:T(8,128)(2,1)} %refs_0_.1), channel_id=1, source_target_pairs={{3,0},{0,1},{1,2},{2,3},{7,4},{4,5},{5,6},{6,7},{11,8},{8,9},{9,10... | collective-permute-start | bytes 393224 | tf_op jit(solution)/shard_map/ppermute | solution.py:236
  9.9 0.0 collective-permute-done.4
  9.9 0.0 collective-permute-done.3
  9.9 0.1 compare_select_fusion.refs_2_
  10.0 0.0 copy-start
  10.0 2.4 %collective-permute-start.6 = (bf16[128,512]{1,0:T(8,128)(2,1)S(1)}, bf16[128,512]{1,0:T(8,128)(2,1)S(1)}, u32[]{:S(2)}, u32[]{:S(2)}) collective-permute-start(bf16[128,512]{1,0:T(8,128)(2,1)S(1)} %compare_select_fusion.refs_2_), channel_id=1, source_target_pairs={{16,0},{20,4},{24,8},{28,12},{0,16},{4,20},{8,24},{12,28},{17,1},{... | collective-permute-start | bytes 393224 | tf_op jit(solution)/shard_map/ppermute | solution.py:260
  12.4 4.3 %collective-permute-start.7 = (bf16[128,512]{1,0:T(8,128)(2,1)S(1)}, bf16[128,512]{1,0:T(8,128)(2,1)S(1)}, u32[]{:S(2)}, u32[]{:S(2)}) collective-permute-start(bf16[128,512]{1,0:T(8,128)(2,1)S(1)} %compare_select_fusion.refs_2_), channel_id=1, source_target_pairs={{0,0},{4,1},{8,2},{12,3},{16,4},{20,5},{24,6},{28,7},{1,8},{5,9},{... | collective-permute-start | bytes 393224 | tf_op jit(solution)/shard_map/ppermute | solution.py:255
  16.7 0.0 collective-permute-done.refs_1_
  16.7 0.0 collective-permute-done.1.refs_2_
  16.8 0.0 collective-permute-done.2.refs_3_
  16.8 17.5 %factor.1 = (f32[512,128]{1,0:T(8,128)}, bf16[512,512]{1,0:T(8,128)(2,1)S(1)}, bf16[512,512]{1,0:T(8,128)(2,1)S(1)}) custom-call(bf16[512,128]{1,0:T(8,128)(2,1)S(1)} %copy-done.1, bf16[512,128]{1,0:T(8,128)(2,1)S(1)} %collective-permute-done.refs_1_, bf16[512,128]{1,0:T(8,128)(2,1)S(1)} %collective-permute-done.1.refs_2_, ...), custom_call_target="tpu_custom_call" | custom-call | flops 1000000000 | bytes 2000000 | tf_op jit(solution)/shard_map/factor/pallas_call | solution.py:267
  34.3 0.0 collective-permute-done.6.refs_3_
  34.3 0.0 collective-permute-done.7.refs_4_
  34.3 1.5 %solve.1 = (bf16[1,32,512]{2,1,0:T(8,128)(2,1)}, bf16[256,128]{1,0:T(8,128)(2,1)}) custom-call(bf16[512,512]{1,0:T(8,128)(2,1)S(1)} %get-tuple-element.9.refs_0_, bf16[512,512]{1,0:T(8,128)(2,1)S(1)} %get-tuple-element.10.refs_1_, bf16[128,512]{1,0:T(8,128)(2,1)S(1)} %compare_select_fusion.refs_2_, bf16[128,512]{1,0:T(8,128)(2,1)S(1)} %collective-permute-done.6.refs_3_, ...), custom_call_target="tpu_custom_call" | custom-call | flops 400000000 | bytes 2000000 | tf_op jit(solution)/shard_map/solve/pallas_call | solution.py:286
  (8 shorter events, 0.0 us)
Async XLA Ops:
  0.6 9.3 %copy-start.2 = (bf16[1,32,512]{2,1,0:T(8,128)(2,1)S(1)}, bf16[1,32,512]{2,1,0:T(8,128)(2,1)}, u32[]{:S(2)}) copy-start(bf16[1,32,512]{2,1,0:T(8,128)(2,1)} %param.5) | copy-start | bytes 98308
  0.6 16.1 %collective-permute-start = (bf16[512,128]{1,0:T(8,128)(2,1)}, bf16[512,128]{1,0:T(8,128)(2,1)S(1)}, u32[]{:S(2)}, u32[]{:S(2)}) collective-permute-start(bf16[512,128]{1,0:T(8,128)(2,1)} %refs_0_.1), channel_id=1, source_target_pairs={{1,0},{2,1},{3,2},{0,3},{5,4},{6,5},{7,6},{4,7},{9,8},{10,9},{11,1... | collective-permute-start | bytes 393224 | tf_op jit(solution)/shard_map/ppermute | solution.py:236
  0.7 16.0 %collective-permute-start.1 = (bf16[512,128]{1,0:T(8,128)(2,1)}, bf16[512,128]{1,0:T(8,128)(2,1)S(1)}, u32[]{:S(2)}, u32[]{:S(2)}) collective-permute-start(bf16[512,128]{1,0:T(8,128)(2,1)} %refs_0_.1), channel_id=1, source_target_pairs={{2,0},{3,1},{0,2},{1,3},{6,4},{7,5},{4,6},{5,7},{10,8},{11,9},{8,1... | collective-permute-start | bytes 393224 | tf_op jit(solution)/shard_map/ppermute | solution.py:236
  3.4 3.9 %collective-permute-start.5 = (bf16[32,512]{1,0:T(8,128)(2,1)}, bf16[32,512]{1,0:T(8,128)(2,1)S(1)}, u32[]{:S(2)}, u32[]{:S(2)}) collective-permute-start(bf16[32,512]{1,0:T(8,128)(2,1)} %bitcast.2), channel_id=1, source_target_pairs={{12,0},{8,4},{4,8},{0,12},{28,16},{24,20},{20,24},{16,28},{13,1},{... | collective-permute-start | bytes 98312 | tf_op jit(solution)/shard_map/ppermute | solution.py:258
  5.7 4.2 %collective-permute-start.4 = (bf16[32,512]{1,0:T(8,128)(2,1)}, bf16[32,512]{1,0:T(8,128)(2,1)S(1)}, u32[]{:S(2)}, u32[]{:S(2)}) collective-permute-start(bf16[32,512]{1,0:T(8,128)(2,1)} %bitcast.3), channel_id=1, source_target_pairs={{8,0},{12,4},{0,8},{4,12},{24,16},{28,20},{16,24},{20,28},{9,1},{1... | collective-permute-start | bytes 98312 | tf_op jit(solution)/shard_map/ppermute | solution.py:258
  5.8 4.0 %collective-permute-start.3 = (bf16[32,512]{1,0:T(8,128)(2,1)}, bf16[32,512]{1,0:T(8,128)(2,1)S(1)}, u32[]{:S(2)}, u32[]{:S(2)}) collective-permute-start(bf16[32,512]{1,0:T(8,128)(2,1)} %bitcast.4), channel_id=1, source_target_pairs={{4,0},{0,4},{12,8},{8,12},{20,16},{16,20},{28,24},{24,28},{5,1},{1... | collective-permute-start | bytes 98312 | tf_op jit(solution)/shard_map/ppermute | solution.py:258
  6.2 0.7 %copy-start.3 = (s32[1,2]{1,0:T(1,128)S(1)}, s32[1,2]{1,0:T(1,128)}, u32[]{:S(2)}) copy-start(s32[1,2]{1,0:T(1,128)} %param.6) | copy-start | bytes 28
  6.9 9.8 %copy-start.1 = (bf16[512,128]{1,0:T(8,128)(2,1)S(1)}, bf16[512,128]{1,0:T(8,128)(2,1)}, u32[]{:S(2)}) copy-start(bf16[512,128]{1,0:T(8,128)(2,1)} %refs_0_.1) | copy-start | bytes 393220
  7.3 9.5 %collective-permute-start.2 = (bf16[512,128]{1,0:T(8,128)(2,1)}, bf16[512,128]{1,0:T(8,128)(2,1)S(1)}, u32[]{:S(2)}, u32[]{:S(2)}) collective-permute-start(bf16[512,128]{1,0:T(8,128)(2,1)} %refs_0_.1), channel_id=1, source_target_pairs={{3,0},{0,1},{1,2},{2,3},{7,4},{4,5},{5,6},{6,7},{11,8},{8,9},{9,10... | collective-permute-start | bytes 393224 | tf_op jit(solution)/shard_map/ppermute | solution.py:236
  10.0 24.3 %copy-start = (bf16[256,128]{1,0:T(8,128)(2,1)S(1)}, bf16[256,128]{1,0:T(8,128)(2,1)}, u32[]{:S(2)}) copy-start(bf16[256,128]{1,0:T(8,128)(2,1)} %refs_5_.1) | copy-start | bytes 196612
  10.0 24.3 %collective-permute-start.6 = (bf16[128,512]{1,0:T(8,128)(2,1)S(1)}, bf16[128,512]{1,0:T(8,128)(2,1)S(1)}, u32[]{:S(2)}, u32[]{:S(2)}) collective-permute-start(bf16[128,512]{1,0:T(8,128)(2,1)S(1)} %compare_select_fusion.refs_2_), channel_id=1, source_target_pairs={{16,0},{20,4},{24,8},{28,12},{0,16},{4,20},{8,24},{12,28},{17,1},{... | collective-permute-start | bytes 393224 | tf_op jit(solution)/shard_map/ppermute | solution.py:260
  12.4 21.9 %collective-permute-start.7 = (bf16[128,512]{1,0:T(8,128)(2,1)S(1)}, bf16[128,512]{1,0:T(8,128)(2,1)S(1)}, u32[]{:S(2)}, u32[]{:S(2)}) collective-permute-start(bf16[128,512]{1,0:T(8,128)(2,1)S(1)} %compare_select_fusion.refs_2_), channel_id=1, source_target_pairs={{0,0},{4,1},{8,2},{12,3},{16,4},{20,5},{24,6},{28,7},{1,8},{5,9},{... | collective-permute-start | bytes 393224 | tf_op jit(solution)/shard_map/ppermute | solution.py:255
where the time goes:
time: 35.9 us; the launch traced here: 35.8 us
  Pallas kernels  19 us (53%)
  starting transfers between devices  14.7 us (41%)
  between operations  0.72 us (2%)
  local copies, waits for them, and re-layouts  0.67 us (2%)
  waiting for transfers between devices  0.39 us (1%)
    pallas_call x1, Pallas kernels, body(): pl.pallas_call(functools.partial(factor_kernel, 'row'), out_shape=(jax.Sh...  17.5 us
    ppermute x3, starting transfers between devices, body(): lax.ppermute(pivot_block, 'row', [((d + s) % rows, d) for d in range(rows)])  5.37 us
    ppermute x1, starting transfers between devices, to_side(): return lax.ppermute(array, ('col', 'row'), pairs)  4.33 us
    ppermute x3, starting transfers between devices, body(): lax.ppermute(panel[0], 'col', [(d ^ p, d) for d in range(cols)])  2.65 us
    ppermute x1, starting transfers between devices, body(): lax.ppermute(quad, 'col', [(d ^ rows, d) for d in range(cols)])  2.38 us
    pallas_call x1, Pallas kernels, body(): pl.pallas_call(functools.partial(solve_kernel, 'row', 'col', True if pair...  1.45 us
  transfers between devices with their start and end apart: 8, of which 1 were waited for; matrix products, arithmetic and copies ran while one was open for 1% of the time, Pallas kernels for 49%

commit v1 on v0

--- a/solution.py
+++ b/solution.py
@@ -93,74 +93,95 @@
     return jnp.concatenate([high, high, low, jnp.zeros_like(high)], axis=0)
 
 
-def factor_kernel(axis, *refs):
+def rows_at(block):
+    return pl.ds(pl.multiple_of(block * LANES, LANES), LANES)
+
+
+def square_iota(axis):
+    return lax.broadcasted_iota(jnp.int32, (LANES, LANES), axis)
+
+
+def beyond_strip():
+    return square_iota(1) // STRIP > square_iota(0) // STRIP
+
+
+def eliminate_block(rows, lower_ref):
+    lane = square_iota(1)
+    done = [[] for _ in rows]
+    for first in range(0, LANES, STRIP):
+        last = first + STRIP
+        solved, diagonal = eliminate_strip(rows[0][:STRIP], first)
+        lower_ref[first:last, :] = diagonal
+        in_strip = (lane[:STRIP] >= first) & (lane[:STRIP] < last)
+        high, low = split(jnp.where(in_strip, solved, 0.0))
+        high, low = high.astype(jnp.float32), low.astype(jnp.float32)
+        inverse = high if first == 0 else pltpu.roll(high, LANES - first, 1)
+        inverse += pltpu.roll(low, (LANES + STRIP - first) % LANES, 1) if first != STRIP else low
+        inverse += pltpu.roll(high, (LANES + 2 * STRIP - first) % LANES, 1) if first != 2 * STRIP else high
+        inverse = inverse.astype(jnp.bfloat16)
+        strips = [solved] + [matmul(inverse, stacked(part[:STRIP])) for part in rows[1:]]
+        for part, strip in zip(done, strips):
+            part.append(strip)
+        if last == LANES:
+            break
+        high, low = split(solved)
+        wide = jnp.concatenate([high, low, high, jnp.zeros_like(high)], axis=0).astype(jnp.float32)
+        left = wide.T[last:, :].astype(jnp.bfloat16)
+        under = [part[STRIP:] for part in rows]
+        inside = (lane[last:] >= first) & (lane[last:] < last)
+        under[0] = jnp.where(inside, 0.0, under[0])
+        rows = [part - matmul(left, stacked(strip)) for part, strip in zip(under, strips)]
+    return [jnp.concatenate(part, axis=0) for part in done]
+
+
+def first_kernel(axis, *refs):
     count = lax.axis_size(axis)
-    parts, (own_ref, high_ref, low_ref, work, lower) = refs[:count], refs[count:]
+    parts, (done_ref, lower_ref, work) = refs[:count], refs[count:]
     me = lax.axis_index(axis)
-    lane = lax.broadcasted_iota(jnp.int32, (LANES, LANES), 1)
-    row = lax.broadcasted_iota(jnp.int32, (LANES, LANES), 0)
-    beyond = lane // STRIP > row // STRIP
     for shift, part in enumerate(parts):
-        work[lax.rem(me + shift, count), : count * LANES, :] = part[...].astype(jnp.float32)
-
-    def rows_at(block):
-        return pl.ds(pl.multiple_of(block * LANES, LANES), LANES)
-
-    def update(target, left, rights, places, on):
-        high, low = split(jnp.where(on, left.T, 0.0))
-        both = jnp.concatenate([high, low], axis=1)
-        for d, (place, (right_high, right_low)) in enumerate(zip(places, rights)):
-            product = matmul(both, jnp.concatenate([right_high, right_high], axis=0)) + matmul(high, right_low)
-            old = work[place, rows_at(target), :]
-            if d == 0:
-                old = jnp.where(on, 0.0, old)
-            work[place, rows_at(target), :] = old - product
+        work[lax.rem(me + shift, count)] = part[:LANES, :].astype(jnp.float32)
+    done = eliminate_block([work[d] for d in range(count)], lower_ref)
+    for d in range(count):
+        done_ref[d] = done[d]
+
+
+def rest_kernel(axis, *refs):
+    count = lax.axis_size(axis)
+    parts, (done_ref, first_lower, own_ref, high_ref, low_ref, work, lower) = refs[:count], refs[count:]
+    me = lax.axis_index(axis)
+    lane, row = square_iota(1), square_iota(0)
+    beyond = beyond_strip()
+    for shift, part in enumerate(parts):
+        work[lax.rem(me + shift, count), LANES : count * LANES, :] = part[LANES:, :].astype(jnp.float32)
+    work[:count, :LANES, :] = done_ref[...]
+    lower[0] = first_lower[...]
 
     def block_step(q, carry):
-        places = [lax.rem(q + d, count) for d in range(count)]
-        rows = [work[place, rows_at(q), :] for place in places]
-
-        before = jnp.maximum(q - 1, 0)
-        old_places = [lax.rem(before + d, count) for d in range(count)]
-        rights = [work[place, rows_at(before), :] for place in old_places]
+        before = q - 1
+        places = [lax.rem(before + d, count) for d in range(count)]
+        rights = [work[place, rows_at(before), :] for place in places]
         rights[0] = jnp.where(beyond, 0.0, rights[0])
         rights = [split(right) for right in rights]
+
+        def update(target):
+            high, low = split(work[target, rows_at(before), :].T)
+            both = jnp.concatenate([high, low], axis=1)
+            new = []
+            for d, (place, (right_high, right_low)) in enumerate(zip(places, rights)):
+                product = matmul(both, jnp.concatenate([right_high, right_high], axis=0)) + matmul(high, right_low)
+                new.append(-product if d == 0 else work[place, rows_at(target), :] - product)
+            return new
+
+        rows = update(q)
         for target in (q + 1, q + 2):
-            update(target, work[target, rows_at(before), :], rights, old_places, q > 0)
-
-        done = [[] for _ in places]
-        for first in range(0, LANES, STRIP):
-            last = first + STRIP
-            solved, diagonal = eliminate_strip(rows[0][:STRIP], first)
-            lower[q, first:last, :] = diagonal
-            in_strip = (lane[:STRIP] >= first) & (lane[:STRIP] < last)
-            high, low = split(jnp.where(in_strip, solved, 0.0))
-            high, low = high.astype(jnp.float32), low.astype(jnp.float32)
-            inverse = high if first == 0 else pltpu.roll(high, LANES - first, 1)
-            inverse += pltpu.roll(low, (LANES + STRIP - first) % LANES, 1) if first != STRIP else low
-            inverse += pltpu.roll(high, (LANES + 2 * STRIP - first) % LANES, 1) if first != 2 * STRIP else high
-            inverse = inverse.astype(jnp.bfloat16)
-            strips = [solved] + [matmul(inverse, stacked(part[:STRIP])) for part in rows[1:]]
-            for part, strip in zip(done, strips):
-                part.append(strip)
-            if last == LANES:
-                break
-            high, low = split(solved)
-            wide = jnp.concatenate([high, low, high, jnp.zeros_like(high)], axis=0).astype(jnp.float32)
-            left = wide.T[last:, :].astype(jnp.bfloat16)
-            under = [part[STRIP:] for part in rows]
-            inside = (lane[last:] >= first) & (lane[last:] < last)
-            under[0] = jnp.where(inside, 0.0, under[0])
-            rows = [part - matmul(left, stacked(strip)) for part, strip in zip(under, strips)]
-
-        done = [jnp.concatenate(part, axis=0) for part in done]
-        for place, part in zip(places, done):
+            for place, new in zip(places, update(target)):
+                work[place, rows_at(target), :] = new
+        done = eliminate_block(rows[1:] + rows[:1], lower.at[q])
+        for place, part in zip(places[1:] + places[:1], done):
             work[place, rows_at(q), :] = part
-        rights = [split(part) for part in [jnp.where(beyond, 0.0, done[0])] + done[1:]]
-        update(q + 1, done[1], rights, places, True)
         return carry
 
-    lax.fori_loop(0, count, block_step, 0)
+    lax.fori_loop(1, count, block_step, 0)
 
     for i in range(count):
         block = work[i, rows_at(me), :]
@@ -236,6 +257,20 @@
         lax.ppermute(pivot_block, "row", [((d + s) % rows, d) for d in range(rows)]) for s in range(1, rows)
     ]
 
+    done, first_lower = pl.pallas_call(
+        functools.partial(first_kernel, "row"),
+        out_shape=(
+            jax.ShapeDtypeStruct((rows, LANES, LANES), jnp.float32),
+            jax.ShapeDtypeStruct((LANES, LANES), jnp.float32),
+        ),
+        in_specs=[vmem] * rows,
+        out_specs=(vmem,) * 2,
+        scratch_shapes=[pltpu.VMEM((rows, LANES, LANES), jnp.float32)],
+        compiler_params=pltpu.CompilerParams(vmem_limit_bytes=32 * 1024 * 1024),
+        cost_estimate=pl.CostEstimate(flops=3 * 10**8, bytes_accessed=10**6, transcendentals=10**5),
+        name="first",
+    )(*pivots)
+
     def live(shards, rows_of):
         block = jnp.concatenate([(shard * share + jnp.arange(share)) // BLOCK for shard in shards])
         matches = block[:, None] == jnp.arange(lead.shape[1])[None, :]
@@ -255,7 +290,12 @@
         return lax.ppermute(array, ("col", "row"), pairs)
 
     if paired:
-        quad = [panel[0]] + [lax.ppermute(panel[0], "col", [(d ^ p, d) for d in range(cols)]) for p in range(1, rows)]
+        own_rows, quad = panel[0], [panel[0]]
+        for p in range(1, rows):
+            if p == rows - 1:
+                own_rows, _ = lax.optimization_barrier((own_rows, pivots))
+            quad.append(lax.ppermute(own_rows, "col", [(d ^ p, d) for d in range(cols)]))
+        quad, _ = lax.optimization_barrier((quad, first_lower))
         quad = live([col_index ^ p for p in range(rows)], jnp.concatenate(quad, axis=0))
         group = [quad, lax.ppermute(quad, "col", [(d ^ rows, d) for d in range(cols)])]
         side = to_side(quad, 0)
@@ -265,13 +305,13 @@
         side = jnp.concatenate([to_side(masked, s) for s in range(rows)], axis=0)
 
     own, high, low = pl.pallas_call(
-        functools.partial(factor_kernel, "row"),
+        functools.partial(rest_kernel, "row"),
         out_shape=(
             jax.ShapeDtypeStruct((pivot_size, local_width), jnp.float32),
             jax.ShapeDtypeStruct((pivot_size, pivot_size), jnp.bfloat16),
             jax.ShapeDtypeStruct((pivot_size, pivot_size), jnp.bfloat16),
         ),
-        in_specs=[vmem] * rows,
+        in_specs=[vmem] * (rows + 2),
         out_specs=(vmem,) * 3,
         scratch_shapes=[
             pltpu.VMEM((rows + 2, pivot_size + 2 * LANES, LANES), jnp.float32),
@@ -279,8 +319,8 @@
         ],
         compiler_params=pltpu.CompilerParams(vmem_limit_bytes=32 * 1024 * 1024),
         cost_estimate=pl.CostEstimate(flops=10**9, bytes_accessed=2 * 10**6, transcendentals=10**5),
-        name="factor",
-    )(*pivots)
+        name="rest",
+    )(*pivots, done, first_lower)
 
     group_rows = share * cols
     panel_factor, schur = pl.pallas_call(

time: 35.9 us -> 37.4 us (1.042)
  waiting for transfers between devices: 0.39 us -> 1.61 us
  Pallas kernels: 19 us -> 17.9 us
  local copies, waits for them, and re-layouts: 0.67 us -> 1.57 us
  starting transfers between devices: 14.7 us -> 15.1 us
    ppermute x3, starting transfers between devices: 2.65 us -> 4.79 us  [body(): lax.ppermute(own_rows, 'col', [(d ^ p, d) for d in range(cols)])]
    ppermute x3, waiting for transfers between devices: 0.01 us -> 1.6 us  [body(): lax.ppermute(pivot_block, 'row', [((d + s) % rows, d) for d in range(rows)])]
    ppermute x3, starting transfers between devices: 5.37 us -> 4.12 us  [body(): lax.ppermute(pivot_block, 'row', [((d + s) % rows, d) for d in range(rows)])]
    pallas_call x1 -> x2, Pallas kernels: 17.5 us -> 16.5 us  [the longest x1 12.8 us: body(): pl.pallas_call(functools.partial(rest_kernel, 'row'), out_shape=(jax.Shap...]
    unnamed x8, local copies, waits for them, and re-layouts: 0.67 us -> 1.57 us
    ppermute x1, starting transfers between devices: 4.33 us -> 3.82 us  [to_side(): return lax.ppermute(array, ('col', 'row'), pairs)]
  transfers between devices with their start and end apart: 8 -> 8, of which waited for: 1 -> 1; matrix products, arithmetic and copies ran while one was open for 1% -> 1% of each run, Pallas kernels for 49% -> 44%
where the time goes in v1:
time: 37.4 us; the launch traced here: 37.2 us
  Pallas kernels  17.9 us (48%)
  starting transfers between devices  15.1 us (40%)
  waiting for transfers between devices  1.61 us (4%)
  local copies, waits for them, and re-layouts  1.57 us (4%)
  between operations  0.7 us (2%)
    pallas_call x1, Pallas kernels, body(): pl.pallas_call(functools.partial(rest_kernel, 'row'), out_shape=(jax.Shap...  12.8 us
    ppermute x3, starting transfers between devices, body(): lax.ppermute(own_rows, 'col', [(d ^ p, d) for d in range(cols)])  4.79 us
    ppermute x3, starting transfers between devices, body(): lax.ppermute(pivot_block, 'row', [((d + s) % rows, d) for d in range(rows)])  4.12 us
    ppermute x1, starting transfers between devices, to_side(): return lax.ppermute(array, ('col', 'row'), pairs)  3.82 us
    pallas_call x1, Pallas kernels, body(): pl.pallas_call(functools.partial(first_kernel, 'row'), out_shape=(jax.Sha...  3.66 us
    ppermute x1, starting transfers between devices, body(): lax.ppermute(quad, 'col', [(d ^ rows, d) for d in range(cols)])  2.38 us
    ppermute x3, waiting for transfers between devices, body(): lax.ppermute(pivot_block, 'row', [((d + s) % rows, d) for d in range(rows)])  1.6 us
    unnamed x8, local copies, waits for them, and re-layouts  1.57 us
  transfers between devices with their start and end apart: 8, of which 1 were waited for; matrix products, arithmetic and copies ran while one was open for 1% of the time, Pallas kernels for 44%

profile of v1, /device:TPU:1, one launch (start us, length us, event | category | flops | bytes accessed | tf_op | source)
XLA Modules:
  0.0 37.2 jit_solution(4080175017655520069)
XLA Ops:
  0.6 0.1 collective-permute-start
  0.7 2.7 %collective-permute-start.1 = (bf16[512,128]{1,0:T(8,128)(2,1)}, bf16[512,128]{1,0:T(8,128)(2,1)S(1)}, u32[]{:S(2)}, u32[]{:S(2)}) collective-permute-start(bf16[512,128]{1,0:T(8,128)(2,1)} %refs_0_.3), channel_id=1, source_target_pairs={{2,0},{3,1},{0,2},{1,3},{6,4},{7,5},{4,6},{5,7},{10,8},{11,9},{8,1... | collective-permute-start | bytes 393224 | tf_op jit(solution)/shard_map/ppermute | solution.py:257
  3.4 1.3 %collective-permute-start.2 = (bf16[512,128]{1,0:T(8,128)(2,1)}, bf16[512,128]{1,0:T(8,128)(2,1)S(1)}, u32[]{:S(2)}, u32[]{:S(2)}) collective-permute-start(bf16[512,128]{1,0:T(8,128)(2,1)} %refs_0_.3), channel_id=1, source_target_pairs={{3,0},{0,1},{1,2},{2,3},{7,4},{4,5},{5,6},{6,7},{11,8},{8,9},{9,10... | collective-permute-start | bytes 393224 | tf_op jit(solution)/shard_map/ppermute | solution.py:257
  4.8 1.2 %collective-permute-start.3 = (bf16[32,512]{1,0:T(8,128)(2,1)}, bf16[32,512]{1,0:T(8,128)(2,1)S(1)}, u32[]{:S(2)}, u32[]{:S(2)}) collective-permute-start(bf16[32,512]{1,0:T(8,128)(2,1)} %bitcast.2), channel_id=1, source_target_pairs={{4,0},{0,4},{12,8},{8,12},{20,16},{16,20},{28,24},{24,28},{5,1},{1... | collective-permute-start | bytes 98312 | tf_op jit(solution)/shard_map/ppermute | solution.py:297
  6.0 1.3 %collective-permute-start.4 = (bf16[32,512]{1,0:T(8,128)(2,1)}, bf16[32,512]{1,0:T(8,128)(2,1)S(1)}, u32[]{:S(2)}, u32[]{:S(2)}) collective-permute-start(bf16[32,512]{1,0:T(8,128)(2,1)} %bitcast.3), channel_id=1, source_target_pairs={{8,0},{12,4},{0,8},{4,12},{24,16},{28,20},{16,24},{20,28},{9,1},{1... | collective-permute-start | bytes 98312 | tf_op jit(solution)/shard_map/ppermute | solution.py:297
  7.3 0.1 pad_add_fusion
  7.4 0.7 %copy-done.3 = s32[1,2]{1,0:T(1,128)S(1)} copy-done((s32[1,2]{1,0:T(1,128)S(1)}, s32[1,2]{1,0:T(1,128)}, u32[]{:S(2)}) %copy-start.3) | copy-done | bytes 32
  8.1 0.1 fusion.3
  8.1 0.0 collective-permute-done.refs_1_
  8.2 0.0 collective-permute-done.1.refs_2_
  8.2 1.6 %collective-permute-done.2.refs_3_ = bf16[512,128]{1,0:T(8,128)(2,1)S(1)} collective-permute-done((bf16[512,128]{1,0:T(8,128)(2,1)}, bf16[512,128]{1,0:T(8,128)(2,1)S(1)}, u32[]{:S(2)}, u32[]{:S(2)}) %collective-permute-start.2) | collective-permute-done | bytes 131104 | tf_op jit(solution)/shard_map/ppermute | solution.py:257
  9.8 2.3 %collective-permute-start.5 = (bf16[32,512]{1,0:T(8,128)(2,1)S(1)}, bf16[32,512]{1,0:T(8,128)(2,1)S(1)}, u32[]{:S(2)}, u32[]{:S(2)}) collective-permute-start(bf16[32,512]{1,0:T(8,128)(2,1)S(1)} %bitcast.4), channel_id=1, source_target_pairs={{12,0},{8,4},{4,8},{0,12},{28,16},{24,20},{20,24},{16,28},{13,1},{... | collective-permute-start | bytes 98312 | tf_op jit(solution)/shard_map/ppermute | solution.py:297
  12.0 0.9 %copy-done.1 = bf16[512,128]{1,0:T(8,128)(2,1)S(1)} copy-done((bf16[512,128]{1,0:T(8,128)(2,1)S(1)}, bf16[512,128]{1,0:T(8,128)(2,1)}, u32[]{:S(2)}) %copy-start.1) | copy-done | bytes 131096
  12.9 3.7 %first.1 = (f32[4,128,128]{2,1,0:T(8,128)S(1)}, f32[128,128]{1,0:T(8,128)S(1)}) custom-call(bf16[512,128]{1,0:T(8,128)(2,1)S(1)} %copy-done.1, bf16[512,128]{1,0:T(8,128)(2,1)S(1)} %collective-permute-done.refs_1_, bf16[512,128]{1,0:T(8,128)(2,1)S(1)} %collective-permute-done.1.refs_2_, bf16[512,128]{1,0:T(8,128)(2,1)S(1)} %collective-permute-done.2.refs_3_), custom_call_target="tpu_custom_call" | custom-call | flops 300000000 | bytes 1000000 | tf_op jit(solution)/shard_map/first/pallas_call | solution.py:260
  16.6 0.0 collective-permute-done.3
  16.6 0.0 collective-permute-done.5
  16.6 0.1 compare_select_fusion.refs_2_
  16.7 2.4 %collective-permute-start.6 = (bf16[128,512]{1,0:T(8,128)(2,1)S(1)}, bf16[128,512]{1,0:T(8,128)(2,1)S(1)}, u32[]{:S(2)}, u32[]{:S(2)}) collective-permute-start(bf16[128,512]{1,0:T(8,128)(2,1)S(1)} %compare_select_fusion.refs_2_), channel_id=1, source_target_pairs={{16,0},{20,4},{24,8},{28,12},{0,16},{4,20},{8,24},{12,28},{17,1},{... | collective-permute-start | bytes 393224 | tf_op jit(solution)/shard_map/ppermute | solution.py:300
  19.1 3.8 %collective-permute-start.7 = (bf16[128,512]{1,0:T(8,128)(2,1)S(1)}, bf16[128,512]{1,0:T(8,128)(2,1)S(1)}, u32[]{:S(2)}, u32[]{:S(2)}) collective-permute-start(bf16[128,512]{1,0:T(8,128)(2,1)S(1)} %compare_select_fusion.refs_2_), channel_id=1, source_target_pairs={{0,0},{4,1},{8,2},{12,3},{16,4},{20,5},{24,6},{28,7},{1,8},{5,9},{... | collective-permute-start | bytes 393224 | tf_op jit(solution)/shard_map/ppermute | solution.py:290
  22.9 0.0 copy-start
  22.9 12.8 %rest.1 = (f32[512,128]{1,0:T(8,128)}, bf16[512,512]{1,0:T(8,128)(2,1)S(1)}, bf16[512,512]{1,0:T(8,128)(2,1)S(1)}) custom-call(bf16[512,128]{1,0:T(8,128)(2,1)S(1)} %copy-done.1, bf16[512,128]{1,0:T(8,128)(2,1)S(1)} %collective-permute-done.refs_1_, bf16[512,128]{1,0:T(8,128)(2,1)S(1)} %collective-permute-done.1.refs_2_, ...), custom_call_target="tpu_custom_call" | custom-call | flops 1000000000 | bytes 2000000 | tf_op jit(solution)/shard_map/rest/pallas_call | solution.py:307
  35.7 0.0 collective-permute-done.6.refs_3_
  35.7 0.0 collective-permute-done.7.refs_4_
  35.7 1.4 %solve.1 = (bf16[1,32,512]{2,1,0:T(8,128)(2,1)}, bf16[256,128]{1,0:T(8,128)(2,1)}) custom-call(bf16[512,512]{1,0:T(8,128)(2,1)S(1)} %get-tuple-element.18.refs_0_, bf16[512,512]{1,0:T(8,128)(2,1)S(1)} %get-tuple-element.19.refs_1_, bf16[128,512]{1,0:T(8,128)(2,1)S(1)} %compare_select_fusion.refs_2_, bf16[128,512]{1,0:T(8,128)(2,1)S(1)} %collective-permute-done.6.refs_3_, ...), custom_call_target="tpu_custom_call" | custom-call | flops 400000000 | bytes 2000000 | tf_op jit(solution)/shard_map/solve/pallas_call | solution.py:326
  (9 shorter events, 0.0 us)
Async XLA Ops:
  0.6 9.1 %copy-start.2 = (bf16[1,32,512]{2,1,0:T(8,128)(2,1)S(1)}, bf16[1,32,512]{2,1,0:T(8,128)(2,1)}, u32[]{:S(2)}) copy-start(bf16[1,32,512]{2,1,0:T(8,128)(2,1)} %param.5) | copy-start | bytes 98308
  0.6 7.5 %collective-permute-start = (bf16[512,128]{1,0:T(8,128)(2,1)}, bf16[512,128]{1,0:T(8,128)(2,1)S(1)}, u32[]{:S(2)}, u32[]{:S(2)}) collective-permute-start(bf16[512,128]{1,0:T(8,128)(2,1)} %refs_0_.3), channel_id=1, source_target_pairs={{1,0},{2,1},{3,2},{0,3},{5,4},{6,5},{7,6},{4,7},{9,8},{10,9},{11,1... | collective-permute-start | bytes 393224 | tf_op jit(solution)/shard_map/ppermute | solution.py:257
  0.7 7.4 %collective-permute-start.1 = (bf16[512,128]{1,0:T(8,128)(2,1)}, bf16[512,128]{1,0:T(8,128)(2,1)S(1)}, u32[]{:S(2)}, u32[]{:S(2)}) collective-permute-start(bf16[512,128]{1,0:T(8,128)(2,1)} %refs_0_.3), channel_id=1, source_target_pairs={{2,0},{3,1},{0,2},{1,3},{6,4},{7,5},{4,6},{5,7},{10,8},{11,9},{8,1... | collective-permute-start | bytes 393224 | tf_op jit(solution)/shard_map/ppermute | solution.py:257
  3.4 6.3 %collective-permute-start.2 = (bf16[512,128]{1,0:T(8,128)(2,1)}, bf16[512,128]{1,0:T(8,128)(2,1)S(1)}, u32[]{:S(2)}, u32[]{:S(2)}) collective-permute-start(bf16[512,128]{1,0:T(8,128)(2,1)} %refs_0_.3), channel_id=1, source_target_pairs={{3,0},{0,1},{1,2},{2,3},{7,4},{4,5},{5,6},{6,7},{11,8},{8,9},{9,10... | collective-permute-start | bytes 393224 | tf_op jit(solution)/shard_map/ppermute | solution.py:257
  4.8 11.8 %collective-permute-start.3 = (bf16[32,512]{1,0:T(8,128)(2,1)}, bf16[32,512]{1,0:T(8,128)(2,1)S(1)}, u32[]{:S(2)}, u32[]{:S(2)}) collective-permute-start(bf16[32,512]{1,0:T(8,128)(2,1)} %bitcast.2), channel_id=1, source_target_pairs={{4,0},{0,4},{12,8},{8,12},{20,16},{16,20},{28,24},{24,28},{5,1},{1... | collective-permute-start | bytes 98312 | tf_op jit(solution)/shard_map/ppermute | solution.py:297
  6.0 10.6 %collective-permute-start.4 = (bf16[32,512]{1,0:T(8,128)(2,1)}, bf16[32,512]{1,0:T(8,128)(2,1)S(1)}, u32[]{:S(2)}, u32[]{:S(2)}) collective-permute-start(bf16[32,512]{1,0:T(8,128)(2,1)} %bitcast.3), channel_id=1, source_target_pairs={{8,0},{12,4},{0,8},{4,12},{24,16},{28,20},{16,24},{20,28},{9,1},{1... | collective-permute-start | bytes 98312 | tf_op jit(solution)/shard_map/ppermute | solution.py:297
  7.4 0.7 %copy-start.3 = (s32[1,2]{1,0:T(1,128)S(1)}, s32[1,2]{1,0:T(1,128)}, u32[]{:S(2)}) copy-start(s32[1,2]{1,0:T(1,128)} %param.6) | copy-start | bytes 28
  9.8 6.8 %collective-permute-start.5 = (bf16[32,512]{1,0:T(8,128)(2,1)S(1)}, bf16[32,512]{1,0:T(8,128)(2,1)S(1)}, u32[]{:S(2)}, u32[]{:S(2)}) collective-permute-start(bf16[32,512]{1,0:T(8,128)(2,1)S(1)} %bitcast.4), channel_id=1, source_target_pairs={{12,0},{8,4},{4,8},{0,12},{28,16},{24,20},{20,24},{16,28},{13,1},{... | collective-permute-start | bytes 98312 | tf_op jit(solution)/shard_map/ppermute | solution.py:297
  12.0 0.9 %copy-start.1 = (bf16[512,128]{1,0:T(8,128)(2,1)S(1)}, bf16[512,128]{1,0:T(8,128)(2,1)}, u32[]{:S(2)}) copy-start(bf16[512,128]{1,0:T(8,128)(2,1)} %refs_0_.3) | copy-start | bytes 393220
  16.7 19.0 %collective-permute-start.6 = (bf16[128,512]{1,0:T(8,128)(2,1)S(1)}, bf16[128,512]{1,0:T(8,128)(2,1)S(1)}, u32[]{:S(2)}, u32[]{:S(2)}) collective-permute-start(bf16[128,512]{1,0:T(8,128)(2,1)S(1)} %compare_select_fusion.refs_2_), channel_id=1, source_target_pairs={{16,0},{20,4},{24,8},{28,12},{0,16},{4,20},{8,24},{12,28},{17,1},{... | collective-permute-start | bytes 393224 | tf_op jit(solution)/shard_map/ppermute | solution.py:300
  19.1 16.7 %collective-permute-start.7 = (bf16[128,512]{1,0:T(8,128)(2,1)S(1)}, bf16[128,512]{1,0:T(8,128)(2,1)S(1)}, u32[]{:S(2)}, u32[]{:S(2)}) collective-permute-start(bf16[128,512]{1,0:T(8,128)(2,1)S(1)} %compare_select_fusion.refs_2_), channel_id=1, source_target_pairs={{0,0},{4,1},{8,2},{12,3},{16,4},{20,5},{24,6},{28,7},{1,8},{5,9},{... | collective-permute-start | bytes 393224 | tf_op jit(solution)/shard_map/ppermute | solution.py:290
  22.9 12.8 %copy-start = (bf16[256,128]{1,0:T(8,128)(2,1)S(1)}, bf16[256,128]{1,0:T(8,128)(2,1)}, u32[]{:S(2)}) copy-start(bf16[256,128]{1,0:T(8,128)(2,1)} %refs_5_.1) | copy-start | bytes 196612
